TPU v7x, 128 devices: a whole 4x4x4 slice. The times are simulated.
128 devices in a mesh: rep: 8 (over x_hi, z), tp: 16 (over x_lo, y, core).
Axes of the slice: x: 4 (x_hi: 2, x_lo: 2; x = x_hi * 2 + x_lo), y: 4, z: 4, core: 2. Of those that a mesh axis runs over, the one named last changes fastest.
Arguments:
- inputs: bfloat16 [12288, 2560], P(('rep', 'tp')), may hold values from -6 to 6
- gate_pre: bfloat16 [12288, 14336], P('rep', 'tp'), may hold values from -6 to 6
- grad_hidden: bfloat16 [12288, 14336], P('rep', 'tp'), may hold values from -6 to 6
- up_weight: bfloat16 [8, 2560, 14336], P('rep', None, 'tp'), may hold values from -6 to 6
- momentum: bfloat16 [8, 2560, 14336], P('rep', None, 'tp'), may hold values from -4 to 4
Outputs:
- input_grad: bfloat16 [12288, 2560], P(('rep', 'tp'))
- mixed_weight: bfloat16 [8, 2560, 14336], P('rep', None, 'tp')
- mixed_moment: bfloat16 [8, 2560, 14336], P('rep', None, 'tp')
All inputs are finite; a program needn't handle non-finite values.
Results may differ from a plain program's by a relative error of at most 0.0055.
Values may be sent and summed in bfloat16 or wider, within the bound.
A program may use at most 192 MiB of HBM per device.

v0:
```python
import jax
import jax.numpy as jnp
from jax import lax
from jax.sharding import PartitionSpec as P

momentum_beta = 0.9
learn_rate = 0.1


def from_behind(shard, axis, by):
    length = lax.axis_size(axis)
    return lax.ppermute(shard, axis, [(i, (i + by) % length) for i in range(length)])


def per_device(inputs, gate_pre, grad_hidden, up_weight, momentum):
    multiplier = up_weight.shape[1] ** (-0.5)
    gate_act = jax.nn.silu(gate_pre.astype(jnp.float32))
    grad_up = (grad_hidden.astype(jnp.float32) * gate_act).astype(jnp.bfloat16)
    weight = up_weight[0]
    row_count = inputs.shape[0]
    whole_grad = (
        lax.dot_general(
            grad_up, weight, (((1,), (1,)), ((), ())), preferred_element_type=jnp.float32
        )
        * multiplier
    )
    summed = lax.psum(whole_grad, "tp")
    input_share = lax.dynamic_slice_in_dim(
        summed, lax.axis_index("tp") * row_count, row_count, 0
    ).astype(jnp.bfloat16)
    fresh_moment = (
        momentum_beta * momentum[0].astype(jnp.float32)
        + lax.dot_general(
            lax.all_gather(inputs, "tp", axis=0, tiled=True),
            grad_up,
            (((0,), (0,)), ((), ())),
            preferred_element_type=jnp.float32,
        )
        * multiplier
    ).astype(jnp.bfloat16)
    fresh_weight = (
        weight.astype(jnp.float32) - learn_rate * fresh_moment.astype(jnp.float32)
    ).astype(jnp.bfloat16)
    stacked = jnp.stack((fresh_weight, fresh_moment))
    previous = from_behind(stacked, "rep", 1)
    following = from_behind(stacked, "rep", -1)
    mixed = (
        (previous.astype(jnp.float32) + stacked.astype(jnp.float32) + following.astype(jnp.float32))
        / 3.0
    ).astype(jnp.bfloat16)
    mixed_weight = mixed[0][None]
    mixed_moment = mixed[1][None]
    return (input_share, mixed_weight, mixed_moment)


def solution(mesh):
    in_specs = (
        P(("rep", "tp"), None),
        P("rep", "tp"),
        P("rep", "tp"),
        P("rep", None, "tp"),
        P("rep", None, "tp"),
    )
    out_specs = (P(("rep", "tp"), None), P("rep", None, "tp"), P("rep", None, "tp"))
    return jax.shard_map(
        per_device, mesh=mesh, in_specs=in_specs, out_specs=out_specs, check_vma=False
    )
```

profile of v0, /device:TPU:0, one launch (start us, length us, event | category | flops | bytes accessed | tf_op | source)
XLA Modules:
  0.0 501.4 jit_solution(438638145478729916)
XLA Ops:
  7.2 0.0 copy-start.1
  7.2 0.0 all-gather.2.cloned.1.call-start
  7.2 0.7 all-gather.2.cloned.1.call-update
  7.9 7.4 %copy.8 = bf16[1,2560,896]{1,2,0:T(8,128)(2,1)} copy(bf16[1,2560,896]{2,1,0:T(8,128)(2,1)} %param.8) | data formatting | bytes 9175040 | tf_op args[3]
  15.3 0.0 copy-done.1
  15.3 14.6 %convolution_multiply_fusion = f32[1536,2560]{1,0:T(8,128)} fusion(bf16[1,2560,896]{2,1,0:T(8,128)(2,1)} %param.8, bf16[1536,896]{1,0:T(8,128)(2,1)S(1)} %copy-done.1, bf16[1536,896]{1,0:T(8,128)(2,1)} %param.7), kind=kOutput, calls=%fused_computation.1 | convolution fusion | flops 7061372928 | bytes 25821184 | tf_op jit(solution)/shard_map/dot_general | solution.py:22
  29.9 7.4 %copy.9 = bf16[1,2560,896]{1,2,0:T(8,128)(2,1)} copy(bf16[1,2560,896]{2,1,0:T(8,128)(2,1)} %param.9) | data formatting | bytes 9175040 | tf_op args[4]
  37.3 24.6 %all-gather.2.cloned.1.call-done = bf16[1536,2560]{1,0:T(8,128)(2,1)} async-done(((bf16[96,2560]{1,0:T(8,128)(2,1)}), bf16[1536,2560]{1,0:T(8,128)(2,1)}) %all-gather.2.cloned.1.call-update) | async-done | bytes 7864336 | tf_op jit(solution)/shard_map/all_gather | solution.py:34
  61.8 12.9 %fusion = bf16[2560,896]{0,1:T(8,128)(2,1)S(1)} fusion(bf16[1,2560,896]{1,2,0:T(8,128)(2,1)} %copy.9, bf16[1536,2560]{1,0:T(8,128)(2,1)} %all-gather.2.cloned.1.call-done, bf16[1536,896]{1,0:T(8,128)(2,1)S(1)} %copy-done.1, bf16[1536,896]{1,0:T(8,128)(2,1)} %param.7), kind=kOutput, calls=%fused_computation.4 | convolution fusion | flops 7068909568 | bytes 22544384 | tf_op jit(solution)/shard_map/dot_general | solution.py:33
  74.8 0.0 copy-start
  74.8 7.5 %fusion.6 = bf16[1,2560,896]{1,2,0:T(8,128)(2,1)} fusion(bf16[2560,896]{0,1:T(8,128)(2,1)S(1)} %fusion, bf16[1,2560,896]{1,2,0:T(8,128)(2,1)} %copy.8), kind=kLoop, calls=%fused_computation.13 | loop fusion | flops 11468800 | bytes 13762560 | tf_op jit(solution)/shard_map/stack | solution.py:44
  82.3 0.0 copy-done
  82.3 8.0 %pad_maximum_fusion = bf16[2,2560,896]{1,2,0:T(8,128)(2,1)} fusion(bf16[1,2560,896]{1,2,0:T(8,128)(2,1)} %bitcast.15, bf16[1,2560,896]{1,2,0:T(8,128)(2,1)} %fusion.6), kind=kLoop, calls=%fused_computation.2 | loop fusion | flops 4587520 | bytes 18350080 | tf_op jit(solution)/shard_map/stack | solution.py:44
  90.2 5.4 %collective-permute-start.1 = (bf16[2,2560,896]{1,2,0:T(8,128)(2,1)}, bf16[2,2560,896]{1,2,0:T(8,128)(2,1)}, u32[]{:S(2)}, u32[]{:S(2)}) collective-permute-start(bf16[2,2560,896]{1,2,0:T(8,128)(2,1)} %pad_maximum_fusion), channel_id=1, source_target_pairs={{0,112},{16,0},{32,16},{48,32},{64,48},{80,64},{96,80},{112,96},{1... | collective-permute-start | bytes 27525128 | tf_op jit(solution)/shard_map/ppermute | solution.py:12
  95.6 0.0 collective-permute-start
  95.6 367.9 %all-reduce.1 = bf16[1536,2560]{1,0:T(8,128)(2,1)} all-reduce(f32[1536,2560]{1,0:T(8,128)} %convolution_multiply_fusion), channel_id=1, replica_groups=mesh['rep'=8,'tp'=16] {'tp'}, use_global_device_ids=true, to_apply=%region_0.1 | all-reduce | flops 3932160 | bytes 23592960 | tf_op jit(solution)/shard_map/psum | solution.py:27
  463.5 1.8 dynamic-slice_convert_fusion
  465.4 0.0 collective-permute-done.1
  465.4 0.0 collective-permute-done
  465.4 10.6 %multiply_convert_fusion = bf16[2,2560,896]{1,2,0:T(8,128)(2,1)S(1)} fusion(bf16[2,2560,896]{1,2,0:T(8,128)(2,1)} %collective-permute-done.1, bf16[2,2560,896]{1,2,0:T(8,128)(2,1)} %collective-permute-done, bf16[1,2560,896]{1,2,0:T(8,128)(2,1)} %bitcast.16, bf16[1,2560,896]{1,2,0:T(8,128)(2,1)} %fusion.6), kind=kLoop, calls=%fused_computation | loop fusion | flops 36700160 | bytes 36700160 | tf_op jit(solution)/shard_map/convert_element_type | solution.py:50
  476.0 4.2 fusion.10
  480.2 7.2 %copy.10 = bf16[1,2560,896]{2,1,0:T(8,128)(2,1)} copy(bf16[1,2560,896]{1,2,0:T(8,128)(2,1)} %get-tuple-element.7) | data formatting | bytes 9175040
  487.4 7.2 %copy.11 = bf16[1,2560,896]{2,1,0:T(8,128)(2,1)} copy(bf16[1,2560,896]{1,2,0:T(8,128)(2,1)} %get-tuple-element.6) | data formatting | bytes 9175040
Async XLA Ops:
  7.2 8.1 %copy-start.1 = (bf16[1536,896]{1,0:T(8,128)(2,1)S(1)}, bf16[1536,896]{1,0:T(8,128)(2,1)}, u32[]{:S(2)}) copy-start(bf16[1536,896]{1,0:T(8,128)(2,1)} %param.6) | copy-start | bytes 8257540
  7.2 54.7 %all-gather.2.cloned.1.call-start = ((), (), s32[]{:S(2)}) async-start(), calls=%async_computation | async-start | bytes 8355840 | tf_op jit(solution)/shard_map/all_gather | solution.py:34
  74.8 7.5 %copy-start = (bf16[2560,896]{0,1:T(8,128)(2,1)}, bf16[2560,896]{0,1:T(8,128)(2,1)S(1)}, u32[]{:S(2)}) copy-start(bf16[2560,896]{0,1:T(8,128)(2,1)S(1)} %fusion) | copy-start | bytes 13762564
  90.2 375.1 %collective-permute-start.1 = (bf16[2,2560,896]{1,2,0:T(8,128)(2,1)}, bf16[2,2560,896]{1,2,0:T(8,128)(2,1)}, u32[]{:S(2)}, u32[]{:S(2)}) collective-permute-start(bf16[2,2560,896]{1,2,0:T(8,128)(2,1)} %pad_maximum_fusion), channel_id=1, source_target_pairs={{0,112},{16,0},{32,16},{48,32},{64,48},{80,64},{96,80},{112,96},{1... | collective-permute-start | bytes 27525128 | tf_op jit(solution)/shard_map/ppermute | solution.py:12
  95.6 369.8 %collective-permute-start = (bf16[2,2560,896]{1,2,0:T(8,128)(2,1)}, bf16[2,2560,896]{1,2,0:T(8,128)(2,1)}, u32[]{:S(2)}, u32[]{:S(2)}) collective-permute-start(bf16[2,2560,896]{1,2,0:T(8,128)(2,1)} %pad_maximum_fusion), channel_id=1, source_target_pairs={{0,16},{16,32},{32,48},{48,64},{64,80},{80,96},{96,112},{112,0},{1... | collective-permute-start | bytes 27525128 | tf_op jit(solution)/shard_map/ppermute | solution.py:12
Sparse Core Ops, SparseCore 0:
  9.7 52.0 all-gather.1
where the time goes:
time: 503 us; the launch traced here: 501 us
  blocking collectives  368 us (73%)
  local copies, waits for them, and re-layouts  35.2 us (7%)
  matrix products  27.5 us (5%)
  other arithmetic  26.1 us (5%)
  waiting for transfers between devices  25.2 us (5%)
  between operations  14.1 us (3%)
  starting transfers between devices  5.4 us (1%)
    psum x1, blocking collectives, per_device(): summed = lax.psum(whole_grad, 'tp')  368 us
    unnamed x8, local copies, waits for them, and re-layouts  29.1 us
    all_gather x1, waiting for transfers between devices, per_device(): lax.all_gather(inputs, 'tp', axis=0, tiled=True)  24.6 us
    another operation x2, other arithmetic, per_device(): stacked = jnp.stack((fresh_weight, fresh_moment))  15.5 us
    dot_general x1, matrix products, per_device(): lax.dot_general(grad_up, weight, (((1,), (1,)), ((), ())), preferred_elem...  14.6 us
    dot_general x1, matrix products, per_device(): lax.dot_general(lax.all_gather(inputs, 'tp', axis=0, tiled=True), grad_up...  12.9 us
    convert_element_type x1, other arithmetic, per_device(): mixed = ((previous.astype(jnp.float32) + stacked.astype(jnp.float32) + fo...  10.6 us
  transfers between devices with their start and end apart: 3, of which 1 were waited for; matrix products, arithmetic and copies ran while one was open for 6% of the time, Pallas kernels for 0%

commit v1 on v0

v1 whole, which is shorter than its diff:
```python
import jax
import jax.numpy as jnp
from jax import lax
from jax.experimental import pallas as pl
from jax.experimental.pallas import tpu as pltpu
from jax.sharding import PartitionSpec as P

momentum_beta = 0.9
learn_rate = 0.1
CHUNK = 256
MESH = pl.DeviceIdType.MESH


def kernel(
    x_hbm, a_hbm, h_hbm, w_hbm, m_hbm,
    ig_hbm, mw_hbm, mm_hbm,
    wv, fv, g, xall, part, crecv, yrecv, xsend, xrecv, igv, wp, wn, fp, fn,
    loc, wsem_s, wsem_r, ag_s, ag_r, rs_s, rs_r, f_s, f_r, out_s,
):
    depth, width = wv.shape
    rows = x_hbm.shape[0]
    tokens = g.shape[0]
    chunks = depth // CHUNK
    scale = depth ** (-0.5)
    rep = lax.axis_index("rep")
    tp = lax.axis_index("tp")
    n_rep = lax.axis_size("rep")
    c = lax.rem(tp, 2)
    y = lax.rem(lax.div(tp, 2), 4)
    xl = lax.div(tp, 8)
    nxt = (lax.rem(rep + 1, n_rep), tp)
    prv = (lax.rem(rep + n_rep - 1, n_rep), tp)
    xother = (rep, tp + 8 - 16 * xl)
    cother = (rep, tp + 1 - 2 * c)
    yo = [lax.rem(y + k, 4) for k in (1, 2, 3)]
    yother = [(rep, xl * 8 + yk * 2 + c) for yk in yo]

    def remote(src, dst, s, r, dev):
        return pltpu.make_async_remote_copy(
            src_ref=src, dst_ref=dst, send_sem=s, recv_sem=r, device_id=dev, device_id_type=MESH
        )

    load_a = pltpu.make_async_copy(a_hbm, fv.at[pl.ds(0, tokens)], loc.at[0])
    load_h = pltpu.make_async_copy(h_hbm, g, loc.at[1])
    load_w = pltpu.make_async_copy(w_hbm, wv, loc.at[2])
    load_x = pltpu.make_async_copy(x_hbm, xall.at[xl, y, c], loc.at[3])
    load_m = pltpu.make_async_copy(m_hbm, fv, loc.at[4])
    load_a.start()
    load_h.start()
    load_w.start()
    load_x.start()

    barrier = pltpu.get_barrier_semaphore()
    for dev in [nxt, prv, xother, cother] + yother:
        pl.semaphore_signal(barrier, inc=1, device_id=dev, device_id_type=MESH)
    pl.semaphore_wait(barrier, 7)

    own = xall.at[xl, y, c]
    ag_x = remote(x_hbm, own, ag_s.at[0], ag_r.at[0], xother)
    ag_y0 = [remote(x_hbm, own, ag_s.at[1 + k], ag_r.at[1 + k], yother[k]) for k in range(3)]
    ag_x.start()
    for cp in ag_y0:
        cp.start()
    w_next = remote(w_hbm, wp, wsem_s.at[0], wsem_r.at[0], nxt)
    w_prev = remote(w_hbm, wn, wsem_s.at[1], wsem_r.at[1], prv)
    w_next.start()
    w_prev.start()

    load_a.wait()
    load_h.wait()

    def act(i, _):
        blk = pl.ds(i * 64, 64)
        v = fv[blk].astype(jnp.float32)
        g[blk] = (g[blk].astype(jnp.float32) * (v / (1.0 + jnp.exp(-v)))).astype(jnp.bfloat16)
        return 0

    lax.fori_loop(0, tokens // 64, act, 0)
    load_m.start()

    far = xall.at[1 - xl, y, c]
    ag_x.wait_recv()
    ag_y1 = [remote(far, far, ag_s.at[4 + k], ag_r.at[4 + k], yother[k]) for k in range(3)]
    for cp in ag_y1:
        cp.start()

    load_w.wait()

    def cot(n, _):
        cols = pl.ds(pl.multiple_of(n * CHUNK, CHUNK), CHUNK)
        res = lax.dot_general(
            g[...], wv[cols], (((1,), (1,)), ((), ())), preferred_element_type=jnp.float32
        )
        part[:, :, :, cols] = res.astype(jnp.bfloat16).reshape(8, 2, rows, CHUNK)
        return 0

    lax.fori_loop(0, chunks, cot, 0)
    rs_c = remote(part.at[:, 1 - c], crecv, rs_s.at[0], rs_r.at[0], cother)

    load_x.wait()
    for cp in ag_y0:
        cp.wait_recv()
    ag_c0 = remote(xall.at[xl, :, c], xall.at[xl, :, c], ag_s.at[7], ag_r.at[7], cother)
    ag_c0.start()
    rs_c.start()
    for cp in ag_y1:
        cp.wait_recv()
    ag_c1 = remote(xall.at[1 - xl, :, c], xall.at[1 - xl, :, c], ag_s.at[8], ag_r.at[8], cother)
    ag_c1.start()

    rs_c.wait_recv()

    def add_core(b, _):
        u, v = lax.div(b, 4), lax.rem(b, 4)
        crecv[b] = (part[b, c].astype(jnp.float32) + crecv[b].astype(jnp.float32)).astype(jnp.bfloat16)
        return 0

    lax.fori_loop(0, 8, add_core, 0)
    rs_y = []
    for k in range(3):
        for u in range(2):
            j = 1 + 2 * k + u
            rs_y.append(
                remote(crecv.at[4 * u + yo[k]], yrecv.at[k, u], rs_s.at[j], rs_r.at[j], yother[k])
            )
    for cp in rs_y:
        cp.start()

    ag_c0.wait_recv()
    ag_c1.wait_recv()
    load_m.wait()

    def moment(n, _):
        blk = pl.ds(pl.multiple_of(n * CHUNK, CHUNK), CHUNK)
        xs = xall[:, :, :, :, blk].reshape(tokens, CHUNK)
        delta = lax.dot_general(
            xs, g[...], (((0,), (0,)), ((), ())), preferred_element_type=jnp.float32
        )
        fv[blk] = (momentum_beta * fv[blk].astype(jnp.float32) + delta * scale).astype(jnp.bfloat16)
        remote(fv.at[blk], fp.at[blk], f_s.at[0, n], f_r.at[0, n], nxt).start()
        remote(fv.at[blk], fn.at[blk], f_s.at[1, n], f_r.at[1, n], prv).start()
        return 0

    lax.fori_loop(0, chunks, moment, 0)

    for cp in rs_y:
        cp.wait_recv()

    def over_y(u):
        return (
            crecv[4 * u + y].astype(jnp.float32)
            + yrecv[0, u].astype(jnp.float32)
            + yrecv[1, u].astype(jnp.float32)
            + yrecv[2, u].astype(jnp.float32)
        )

    xsend[...] = over_y(1 - xl).astype(jnp.bfloat16)
    rs_x = remote(xsend, xrecv, rs_s.at[7], rs_r.at[7], xother)
    rs_x.start()
    rs_x.wait_recv()
    igv[...] = ((over_y(xl) + xrecv[...].astype(jnp.float32)) * scale).astype(jnp.bfloat16)
    out_ig = pltpu.make_async_copy(igv, ig_hbm, loc.at[5])
    out_ig.start()

    w_next.wait_recv()
    w_prev.wait_recv()

    def fresh(w, f):
        return (w.astype(jnp.float32) - learn_rate * f).astype(jnp.bfloat16).astype(jnp.float32)

    def mix(n, _):
        blk = pl.ds(pl.multiple_of(n * CHUNK, CHUNK), CHUNK)
        remote(fv.at[blk], fp.at[blk], f_s.at[0, n], f_r.at[0, n], nxt).wait()
        remote(fv.at[blk], fn.at[blk], f_s.at[1, n], f_r.at[1, n], prv).wait()

        def piece(i, _):
            sub = pl.ds(pl.multiple_of(n * CHUNK + i * 32, 32), 32)
            f0, f1, f2 = (r[sub].astype(jnp.float32) for r in (fp, fv, fn))
            w = fresh(wp[sub], f0) + fresh(wv[sub], f1) + fresh(wn[sub], f2)
            wp[sub] = (w / 3.0).astype(jnp.bfloat16)
            fp[sub] = ((f0 + f1 + f2) / 3.0).astype(jnp.bfloat16)
            return 0

        lax.fori_loop(0, CHUNK // 32, piece, 0)
        pltpu.make_async_copy(wp.at[blk], mw_hbm.at[blk], out_s.at[0, n]).start()
        pltpu.make_async_copy(fp.at[blk], mm_hbm.at[blk], out_s.at[1, n]).start()
        return 0

    lax.fori_loop(0, chunks, mix, 0)

    def drain(n, _):
        blk = pl.ds(pl.multiple_of(n * CHUNK, CHUNK), CHUNK)
        pltpu.make_async_copy(wp.at[blk], mw_hbm.at[blk], out_s.at[0, n]).wait()
        pltpu.make_async_copy(fp.at[blk], mm_hbm.at[blk], out_s.at[1, n]).wait()
        return 0

    lax.fori_loop(0, chunks, drain, 0)
    out_ig.wait()
    for cp in [ag_x, *ag_y0, *ag_y1, ag_c0, ag_c1, rs_c, *rs_y, rs_x, w_next, w_prev]:
        cp.wait_send()


def per_device(inputs, gate_pre, grad_hidden, up_weight, momentum):
    rows, depth = inputs.shape
    tokens, width = gate_pre.shape
    chunks = depth // CHUNK
    bf = jnp.bfloat16
    any_spec = pl.BlockSpec(memory_space=pl.ANY)
    dma = pltpu.SemaphoreType.DMA
    big = pltpu.VMEM((depth, width), bf)
    ig, mw, mm = pl.pallas_call(
        kernel,
        out_shape=(
            jax.ShapeDtypeStruct((rows, depth), bf),
            jax.ShapeDtypeStruct((depth, width), bf),
            jax.ShapeDtypeStruct((depth, width), bf),
        ),
        in_specs=[any_spec] * 5,
        out_specs=(any_spec,) * 3,
        scratch_shapes=[
            big,
            big,
            pltpu.VMEM((tokens, width), bf),
            pltpu.VMEM((2, 4, 2, rows, depth), bf),
            pltpu.VMEM((8, 2, rows, depth), bf),
            pltpu.VMEM((8, rows, depth), bf),
            pltpu.VMEM((3, 2, rows, depth), bf),
            pltpu.VMEM((rows, depth), bf),
            pltpu.VMEM((rows, depth), bf),
            pltpu.VMEM((rows, depth), bf),
            big,
            big,
            big,
            big,
            dma((6,)),
            dma((2,)),
            dma((2,)),
            dma((9,)),
            dma((9,)),
            dma((8,)),
            dma((8,)),
            dma((2, chunks)),
            dma((2, chunks)),
            dma((2, chunks)),
        ],
        compiler_params=pltpu.CompilerParams(
            collective_id=0, has_side_effects=True, vmem_limit_bytes=62 * 2**20
        ),
        name="step",
    )(inputs, gate_pre, grad_hidden, up_weight[0], momentum[0])
    return ig, mw[None], mm[None]


def solution(mesh):
    in_specs = (
        P(("rep", "tp"), None),
        P("rep", "tp"),
        P("rep", "tp"),
        P("rep", None, "tp"),
        P("rep", None, "tp"),
    )
    out_specs = (P(("rep", "tp"), None), P("rep", None, "tp"), P("rep", None, "tp"))
    return jax.shard_map(
        per_device, mesh=mesh, in_specs=in_specs, out_specs=out_specs, check_vma=False
    )
```

time: 503 us -> 245 us (0.49)
  blocking collectives: 368 us -> 0 us
  Pallas kernels: 0 us -> 236 us
  matrix products: 27.5 us -> 0 us
  local copies, waits for them, and re-layouts: 35.2 us -> 9 us
  other arithmetic: 26.1 us -> 0.01 us
  waiting for transfers between devices: 25.2 us -> 0 us
  between operations: 14.1 us -> 0.65 us
  starting transfers between devices: 5.4 us -> 0 us
    psum x1 -> x0, blocking collectives: 368 us -> none  [per_device(): summed = lax.psum(whole_grad, 'tp')]
    pallas_call x0 -> x1, Pallas kernels: none -> 236 us  [per_device(): pl.pallas_call(kernel, out_shape=(jax.ShapeDtypeStruct((rows, depth), bf)...]
    dot_general x2 -> x0, matrix products: 27.5 us -> none  [the longest x1 14.6 us: per_device(): lax.dot_general(grad_up, weight, (((1,), (1,)), ((), ())), preferred_elem...]
    all_gather x1 -> x0, waiting for transfers between devices: 24.6 us -> none  [per_device(): lax.all_gather(inputs, 'tp', axis=0, tiled=True)]
    unnamed x8 -> x7, local copies, waits for them, and re-layouts: 29.1 us -> 9 us
    another operation x2 -> x0, other arithmetic: 15.5 us -> none  [per_device(): stacked = jnp.stack((fresh_weight, fresh_moment))]
    convert_element_type x1 -> x0, other arithmetic: 10.6 us -> none  [per_device(): mixed = ((previous.astype(jnp.float32) + stacked.astype(jnp.float32) + fo...]
    ppermute x2 -> x0, starting transfers between devices: 5.37 us -> none  [from_behind(): lax.ppermute(shard, axis, [(i, (i + by) % length) for i in range(length)])]
  transfers between devices with their start and end apart: 3 -> 0, of which waited for: 1 -> 0; matrix products, arithmetic and copies ran while one was open for 6% -> 0% of each run, Pallas kernels for 0% -> 0%
where the time goes in v1:
time: 245 us
  Pallas kernels  236 us (96%)
  local copies, waits for them, and re-layouts  9 us (4%)
    pallas_call x1, Pallas kernels, per_device(): pl.pallas_call(kernel, out_shape=(jax.ShapeDtypeStruct((rows, depth), bf)...  236 us
    unnamed x7, local copies, waits for them, and re-layouts  9 us

profile of v1, /device:TPU:0, one launch (start us, length us, event | category | flops | bytes accessed | tf_op | source)
XLA Modules:
  0.0 245.2 jit_solution(12821631779744697438)
XLA Ops:
  0.6 235.6 %step.1 = (bf16[96,2560]{1,0:T(8,128)(2,1)}, bf16[2560,896]{1,0:T(8,128)(2,1)}, bf16[2560,896]{1,0:T(8,128)(2,1)}) custom-call(bf16[96,2560]{1,0:T(8,128)(2,1)} %x_hbm.1, bf16[1536,896]{1,0:T(8,128)(2,1)} %a_hbm.1, bf16[1536,896]{1,0:T(8,128)(2,1)} %h_hbm.1, bf16[2560,896]{1,0:T(8,128)(2,1)} %bitcast.8, bf16[2560,896]{1,0:T(8,128)(2,1)} %bitcast.9), custom_call_target="tpu_custom_call" | custom-call | tf_op jit(solution)/shard_map/step/pallas_call | solution.py:211
  236.2 0.0 slice-start
  236.2 2.0 copy.11
  238.2 0.0 slice-start.1
  238.2 4.9 %copy.12 = bf16[1,2560,896]{2,1,0:T(8,128)(2,1)} copy(bf16[1,2560,896]{2,1,0:T(8,128)(2,1)} %bitcast.7) | data formatting | bytes 9175040
  243.1 0.0 slice-done
  243.1 0.0 slice-done.1
  243.1 2.1 copy.13
  (1 shorter events, 0.0 us)
Async XLA Ops:
  236.2 6.9 %slice-start = ((s8[4587520]{0:T(1024)(128)(4,1)}), s8[4194304]{0:T(1024)(128)(4,1)S(1)}, s32[]{:S(2)}) async-start(s8[4587520]{0:T(1024)(128)(4,1)} %bitcast.4), calls=%async_computation | async-start | bytes 8388608
  238.2 4.9 %slice-start.1 = ((s8[4587520]{0:T(1024)(128)(4,1)}), s8[393216]{0:T(1024)(128)(4,1)S(1)}, s32[]{:S(2)}) async-start(s8[4587520]{0:T(1024)(128)(4,1)} %bitcast.4), calls=%async_computation.1 | async-start | bytes 786432

commit v2 on v1

--- a/solution.py
+++ b/solution.py
@@ -8,14 +8,20 @@
 momentum_beta = 0.9
 learn_rate = 0.1
 CHUNK = 256
+INNER_ROWS = 512
+OUTER_ROWS = 320
+PIECE = 32
+FIRST = 4
+LATE = 7
 MESH = pl.DeviceIdType.MESH
 
 
 def kernel(
     x_hbm, a_hbm, h_hbm, w_hbm, m_hbm,
     ig_hbm, mw_hbm, mm_hbm,
-    wv, fv, g, xall, part, crecv, yrecv, xsend, xrecv, igv, wp, wn, fp, fn,
-    loc, wsem_s, wsem_r, ag_s, ag_r, rs_s, rs_r, f_s, f_r, out_s,
+    wv, fv, g, xall, part, crecv, yrecv, xsend, xrecv, igv, wn, wo, fn, fo,
+    relw,
+    loc, wsem_s, wsem_r, ag_s, ag_r, rs_s, rs_r, f_s, f_r, rel_s, rel_r, out_s,
 ):
     depth, width = wv.shape
     rows = x_hbm.shape[0]
@@ -24,16 +30,26 @@
     scale = depth ** (-0.5)
     rep = lax.axis_index("rep")
     tp = lax.axis_index("tp")
-    n_rep = lax.axis_size("rep")
     c = lax.rem(tp, 2)
     y = lax.rem(lax.div(tp, 2), 4)
     xl = lax.div(tp, 8)
-    nxt = (lax.rem(rep + 1, n_rep), tp)
-    prv = (lax.rem(rep + n_rep - 1, n_rep), tp)
+    yo = [lax.rem(y + k, 4) for k in (1, 2, 3)]
+    yother = [(rep, xl * 8 + yk * 2 + c) for yk in yo]
+    odd = lax.rem(rep, 2)
+    quad = lax.rem(rep, 4)
+    inner = jnp.logical_or(quad == 1, quad == 2)
+    near = (rep + 1 - 2 * odd, tp)
+    out = (lax.rem(rep + 7 + 2 * odd, 8), tp)
+    across = (jnp.where(inner, 7 - rep, 3 - rep + 8 * lax.div(rep, 4)), tp)
     xother = (rep, tp + 8 - 16 * xl)
     cother = (rep, tp + 1 - 2 * c)
-    yo = [lax.rem(y + k, 4) for k in (1, 2, 3)]
-    yother = [(rep, xl * 8 + yk * 2 + c) for yk in yo]
+    inner_rows = pl.ds(0, INNER_ROWS)
+    outer_rows = pl.ds(INNER_ROWS, OUTER_ROWS)
+    rest = pl.ds(INNER_ROWS + OUTER_ROWS, depth - INNER_ROWS - OUTER_ROWS)
+
+    def by_kind(run):
+        pl.when(inner)(lambda: run(inner_rows, outer_rows))
+        pl.when(jnp.logical_not(inner))(lambda: run(outer_rows, inner_rows))
 
     def remote(src, dst, s, r, dev):
         return pltpu.make_async_remote_copy(
@@ -51,9 +67,9 @@
     load_x.start()
 
     barrier = pltpu.get_barrier_semaphore()
-    for dev in [nxt, prv, xother, cother] + yother:
+    for dev in [near, out, across, xother, cother] + yother:
         pl.semaphore_signal(barrier, inc=1, device_id=dev, device_id_type=MESH)
-    pl.semaphore_wait(barrier, 7)
+    pl.semaphore_wait(barrier, 8)
 
     own = xall.at[xl, y, c]
     ag_x = remote(x_hbm, own, ag_s.at[0], ag_r.at[0], xother)
@@ -61,10 +77,28 @@
     ag_x.start()
     for cp in ag_y0:
         cp.start()
-    w_next = remote(w_hbm, wp, wsem_s.at[0], wsem_r.at[0], nxt)
-    w_prev = remote(w_hbm, wn, wsem_s.at[1], wsem_r.at[1], prv)
-    w_next.start()
-    w_prev.start()
+    w_near = remote(w_hbm.at[rest], wn.at[rest], wsem_s.at[0, 1], wsem_r.at[0, 1], near)
+    w_out = remote(w_hbm.at[rest], wo.at[rest], wsem_s.at[1, 1], wsem_r.at[1, 1], out)
+
+    def near_rows(blk):
+        return remote(w_hbm.at[blk], wn.at[blk], wsem_s.at[0, 0], wsem_r.at[0, 0], near)
+
+    def out_rows(blk):
+        return remote(w_hbm.at[blk], wo.at[blk], wsem_s.at[1, 0], wsem_r.at[1, 0], out)
+
+    def relay(blk):
+        return remote(wn.at[blk], relw.at[pl.ds(0, blk.size)], rel_s.at[0], rel_r.at[0], across)
+
+    def sums(blk):
+        return remote(relw.at[pl.ds(0, blk.size)], wn.at[blk], rel_s.at[1], rel_r.at[1], near)
+
+    def first_rows(mine, theirs):
+        near_rows(theirs).start()
+        out_rows(mine).start()
+
+    by_kind(first_rows)
+    w_near.start()
+    w_out.start()
 
     load_a.wait()
     load_h.wait()
@@ -95,6 +129,12 @@
         return 0
 
     lax.fori_loop(0, chunks, cot, 0)
+
+    def pass_on(mine, theirs):
+        near_rows(mine).wait_recv()
+        relay(mine).start()
+
+    by_kind(pass_on)
     rs_c = remote(part.at[:, 1 - c], crecv, rs_s.at[0], rs_r.at[0], cother)
 
     load_x.wait()
@@ -130,18 +170,56 @@
     ag_c1.wait_recv()
     load_m.wait()
 
-    def moment(n, _):
-        blk = pl.ds(pl.multiple_of(n * CHUNK, CHUNK), CHUNK)
+    def send_near(blk, n):
+        return remote(fv.at[blk], fn.at[blk], f_s.at[0, n], f_r.at[0, n], near)
+
+    def send_out(blk, n):
+        return remote(fv.at[blk], fo.at[blk], f_s.at[1, n], f_r.at[1, n], out)
+
+    def moment(blk):
         xs = xall[:, :, :, :, blk].reshape(tokens, CHUNK)
         delta = lax.dot_general(
             xs, g[...], (((0,), (0,)), ((), ())), preferred_element_type=jnp.float32
         )
         fv[blk] = (momentum_beta * fv[blk].astype(jnp.float32) + delta * scale).astype(jnp.bfloat16)
-        remote(fv.at[blk], fp.at[blk], f_s.at[0, n], f_r.at[0, n], nxt).start()
-        remote(fv.at[blk], fn.at[blk], f_s.at[1, n], f_r.at[1, n], prv).start()
-        return 0
-
-    lax.fori_loop(0, chunks, moment, 0)
+
+    def rows_of(n):
+        return pl.ds(pl.multiple_of(n * CHUNK, CHUNK), CHUNK)
+
+    def moments(n, _):
+        moment(rows_of(n))
+        return 0
+
+    def send(lo, hi, *ways):
+        def go(n, _):
+            for way in ways:
+                way(rows_of(n), n).start()
+            return 0
+
+        lax.fori_loop(lo, hi, go, 0)
+
+    def early(n, _):
+        moments(n, 0)
+        send_near(rows_of(n), n).start()
+        pl.when(inner)(lambda: send_out(rows_of(n), n).start())
+        return 0
+
+    lax.fori_loop(0, FIRST, early, 0)
+    lax.fori_loop(FIRST, chunks, moments, 0)
+
+    def send_sum(mine, theirs):
+        relay(mine).wait_recv()
+
+        def add_own(i, _):
+            here = pl.ds(pl.multiple_of(i * PIECE, PIECE), PIECE)
+            sub = pl.ds(pl.multiple_of(mine.start + i * PIECE, PIECE), PIECE)
+            relw[here] = (relw[here].astype(jnp.float32) + wv[sub].astype(jnp.float32)).astype(jnp.bfloat16)
+            return 0
+
+        lax.fori_loop(0, mine.size // PIECE, add_own, 0)
+        sums(mine).start()
+
+    pl.when(inner)(lambda: send_sum(inner_rows, outer_rows))
 
     for cp in rs_y:
         cp.wait_recv()
@@ -157,46 +235,91 @@
     xsend[...] = over_y(1 - xl).astype(jnp.bfloat16)
     rs_x = remote(xsend, xrecv, rs_s.at[7], rs_r.at[7], xother)
     rs_x.start()
+    pl.when(inner)(lambda: send(FIRST, chunks, send_near, send_out))
+
+    @pl.when(jnp.logical_not(inner))
+    def _():
+        relay(outer_rows).wait_send()
+        send(0, chunks, send_out)
+        send_sum(outer_rows, inner_rows)
+        send(FIRST, chunks, send_near)
+
+    w_near.wait_recv()
+    w_out.wait_recv()
+
+    def last_rows(mine, theirs):
+        out_rows(mine).wait_recv()
+        sums(theirs).wait_recv()
+
+    by_kind(last_rows)
+    pl.when(inner)(lambda: relay(inner_rows).wait_send())
+    low = jnp.where(inner, INNER_ROWS, 0)
+    high = jnp.where(inner, INNER_ROWS + OUTER_ROWS, INNER_ROWS)
+
+    def fresh(w, f):
+        return (w.astype(jnp.float32) - learn_rate * f).astype(jnp.bfloat16).astype(jnp.float32)
+
+    def outputs(n):
+        blk = rows_of(n)
+        return (
+            pltpu.make_async_copy(wn.at[blk], mw_hbm.at[blk], out_s.at[0, n]),
+            pltpu.make_async_copy(fn.at[blk], mm_hbm.at[blk], out_s.at[1, n]),
+        )
+
+    def mix(n, _):
+        blk = rows_of(n)
+        send_near(blk, n).wait_recv()
+        send_out(blk, n).wait_recv()
+
+        def piece(i, _):
+            start = n * CHUNK + i * PIECE
+            sub = pl.ds(pl.multiple_of(start, PIECE), PIECE)
+            summed = jnp.logical_and(start >= low, start < high)
+            f0, f1, f2 = (r[sub].astype(jnp.float32) for r in (fn, fv, fo))
+            own = fresh(wv[sub], f1)
+
+            @pl.when(summed)
+            def _():
+                w = wn[sub].astype(jnp.float32) - learn_rate * (f0 + f2) + own
+                wn[sub] = (w * (1.0 / 3.0)).astype(jnp.bfloat16)
+
+            @pl.when(jnp.logical_not(summed))
+            def _():
+                w = fresh(wn[sub], f0) + own + fresh(wo[sub], f2)
+                wn[sub] = (w * (1.0 / 3.0)).astype(jnp.bfloat16)
+
+            fn[sub] = ((f0 + f1 + f2) * (1.0 / 3.0)).astype(jnp.bfloat16)
+            return 0
+
+        lax.fori_loop(0, CHUNK // PIECE, piece, 0)
+        for cp in outputs(n):
+            cp.start()
+        return 0
+
+    lax.fori_loop(0, LATE, mix, 0)
     rs_x.wait_recv()
     igv[...] = ((over_y(xl) + xrecv[...].astype(jnp.float32)) * scale).astype(jnp.bfloat16)
     out_ig = pltpu.make_async_copy(igv, ig_hbm, loc.at[5])
     out_ig.start()
-
-    w_next.wait_recv()
-    w_prev.wait_recv()
-
-    def fresh(w, f):
-        return (w.astype(jnp.float32) - learn_rate * f).astype(jnp.bfloat16).astype(jnp.float32)
-
-    def mix(n, _):
-        blk = pl.ds(pl.multiple_of(n * CHUNK, CHUNK), CHUNK)
-        remote(fv.at[blk], fp.at[blk], f_s.at[0, n], f_r.at[0, n], nxt).wait()
-        remote(fv.at[blk], fn.at[blk], f_s.at[1, n], f_r.at[1, n], prv).wait()
-
-        def piece(i, _):
-            sub = pl.ds(pl.multiple_of(n * CHUNK + i * 32, 32), 32)
-            f0, f1, f2 = (r[sub].astype(jnp.float32) for r in (fp, fv, fn))
-            w = fresh(wp[sub], f0) + fresh(wv[sub], f1) + fresh(wn[sub], f2)
-            wp[sub] = (w / 3.0).astype(jnp.bfloat16)
-            fp[sub] = ((f0 + f1 + f2) / 3.0).astype(jnp.bfloat16)
-            return 0
-
-        lax.fori_loop(0, CHUNK // 32, piece, 0)
-        pltpu.make_async_copy(wp.at[blk], mw_hbm.at[blk], out_s.at[0, n]).start()
-        pltpu.make_async_copy(fp.at[blk], mm_hbm.at[blk], out_s.at[1, n]).start()
-        return 0
-
-    lax.fori_loop(0, chunks, mix, 0)
+    lax.fori_loop(LATE, chunks, mix, 0)
 
     def drain(n, _):
-        blk = pl.ds(pl.multiple_of(n * CHUNK, CHUNK), CHUNK)
-        pltpu.make_async_copy(wp.at[blk], mw_hbm.at[blk], out_s.at[0, n]).wait()
-        pltpu.make_async_copy(fp.at[blk], mm_hbm.at[blk], out_s.at[1, n]).wait()
+        blk = rows_of(n)
+        send_near(blk, n).wait_send()
+        send_out(blk, n).wait_send()
+        for cp in outputs(n):
+            cp.wait()
         return 0
 
     lax.fori_loop(0, chunks, drain, 0)
     out_ig.wait()
-    for cp in [ag_x, *ag_y0, *ag_y1, ag_c0, ag_c1, rs_c, *rs_y, rs_x, w_next, w_prev]:
+    def sent(mine, theirs):
+        near_rows(theirs).wait_send()
+        out_rows(mine).wait_send()
+        sums(mine).wait_send()
+
+    by_kind(sent)
+    for cp in [ag_x, *ag_y0, *ag_y1, ag_c0, ag_c1, rs_c, *rs_y, rs_x, w_near, w_out]:
         cp.wait_send()
 
 
@@ -232,15 +355,18 @@
             big,
             big,
             big,
+            pltpu.VMEM((max(INNER_ROWS, OUTER_ROWS), width), bf),
             dma((6,)),
-            dma((2,)),
-            dma((2,)),
+            dma((2, 2)),
+            dma((2, 2)),
             dma((9,)),
             dma((9,)),
             dma((8,)),
             dma((8,)),
             dma((2, chunks)),
             dma((2, chunks)),
+            dma((2,)),
+            dma((2,)),
             dma((2, chunks)),
         ],
         compiler_params=pltpu.CompilerParams(

time: 245 us -> 224 us (0.914)
  Pallas kernels: 236 us -> 214 us
    pallas_call x1, Pallas kernels: 236 us -> 214 us  [per_device(): pl.pallas_call(kernel, out_shape=(jax.ShapeDtypeStruct((rows, depth), bf)...]
where the time goes in v2:
time: 224 us; the launch traced here: 223 us
  Pallas kernels  214 us (96%)
  local copies, waits for them, and re-layouts  9 us (4%)
    pallas_call x1, Pallas kernels, per_device(): pl.pallas_call(kernel, out_shape=(jax.ShapeDtypeStruct((rows, depth), bf)...  214 us
    unnamed x7, local copies, waits for them, and re-layouts  9 us

profile of v2, /device:TPU:0, one launch (start us, length us, event | category | flops | bytes accessed | tf_op | source)
XLA Modules:
  0.0 223.3 jit_solution(6407685350422882242)
XLA Ops:
  0.6 213.6 %step.1 = (bf16[96,2560]{1,0:T(8,128)(2,1)}, bf16[2560,896]{1,0:T(8,128)(2,1)}, bf16[2560,896]{1,0:T(8,128)(2,1)}) custom-call(bf16[96,2560]{1,0:T(8,128)(2,1)} %x_hbm.1, bf16[1536,896]{1,0:T(8,128)(2,1)} %a_hbm.1, bf16[1536,896]{1,0:T(8,128)(2,1)} %h_hbm.1, bf16[2560,896]{1,0:T(8,128)(2,1)} %bitcast.8, bf16[2560,896]{1,0:T(8,128)(2,1)} %bitcast.9), custom_call_target="tpu_custom_call" | custom-call | tf_op jit(solution)/shard_map/step/pallas_call | solution.py:334
  214.2 0.0 slice-start
  214.3 2.0 copy.11
  216.2 0.0 slice-start.1
  216.3 4.9 %copy.12 = bf16[1,2560,896]{2,1,0:T(8,128)(2,1)} copy(bf16[1,2560,896]{2,1,0:T(8,128)(2,1)} %bitcast.7) | data formatting | bytes 9175040
  221.1 0.0 slice-done
  221.1 0.0 slice-done.1
  221.1 2.1 copy.13
  (1 shorter events, 0.0 us)
Async XLA Ops:
  214.2 6.9 %slice-start = ((s8[4587520]{0:T(1024)(128)(4,1)}), s8[4194304]{0:T(1024)(128)(4,1)S(1)}, s32[]{:S(2)}) async-start(s8[4587520]{0:T(1024)(128)(4,1)} %bitcast.4), calls=%async_computation | async-start | bytes 8388608
  216.2 4.9 %slice-start.1 = ((s8[4587520]{0:T(1024)(128)(4,1)}), s8[393216]{0:T(1024)(128)(4,1)S(1)}, s32[]{:S(2)}) async-start(s8[4587520]{0:T(1024)(128)(4,1)} %bitcast.4), calls=%async_computation.1 | async-start | bytes 786432

commit v3 on v2

--- a/solution.py
+++ b/solution.py
@@ -8,8 +8,8 @@
 momentum_beta = 0.9
 learn_rate = 0.1
 CHUNK = 256
-INNER_ROWS = 512
-OUTER_ROWS = 320
+INNER_ROWS = (640,)
+OUTER_ROWS = (288, 320)
 PIECE = 32
 FIRST = 4
 LATE = 7
@@ -18,10 +18,10 @@
 
 def kernel(
     x_hbm, a_hbm, h_hbm, w_hbm, m_hbm,
-    ig_hbm, mw_hbm, mm_hbm,
-    wv, fv, g, xall, part, crecv, yrecv, xsend, xrecv, igv, wn, wo, fn, fo,
+    igv, wn, fn,
+    wv, fv, g, xall, part, crecv, yrecv, xsend, xrecv, wo, fo,
     relw,
-    loc, wsem_s, wsem_r, ag_s, ag_r, rs_s, rs_r, f_s, f_r, rel_s, rel_r, out_s,
+    loc, wsem_s, wsem_r, ag_s, ag_r, rs_s, rs_r, f_s, f_r, rel_s, rel_r, grants,
 ):
     depth, width = wv.shape
     rows = x_hbm.shape[0]
@@ -43,9 +43,13 @@
     across = (jnp.where(inner, 7 - rep, 3 - rep + 8 * lax.div(rep, 4)), tp)
     xother = (rep, tp + 8 - 16 * xl)
     cother = (rep, tp + 1 - 2 * c)
-    inner_rows = pl.ds(0, INNER_ROWS)
-    outer_rows = pl.ds(INNER_ROWS, OUTER_ROWS)
-    rest = pl.ds(INNER_ROWS + OUTER_ROWS, depth - INNER_ROWS - OUTER_ROWS)
+    outs = (out, (out[0], cother[1]))
+    inner_rows, outer_rows, at = [], [], 0
+    for sizes, blocks in ((INNER_ROWS, inner_rows), (OUTER_ROWS, outer_rows)):
+        for size in sizes:
+            blocks.append(pl.ds(at, size))
+            at += size
+    rest = pl.ds(at, depth - at)
 
     def by_kind(run):
         pl.when(inner)(lambda: run(inner_rows, outer_rows))
@@ -67,38 +71,75 @@
     load_x.start()
 
     barrier = pltpu.get_barrier_semaphore()
-    for dev in [near, out, across, xother, cother] + yother:
+    for dev in [near, *outs, across, xother, cother] + yother:
         pl.semaphore_signal(barrier, inc=1, device_id=dev, device_id_type=MESH)
-    pl.semaphore_wait(barrier, 8)
+    pl.semaphore_wait(barrier, 9)
 
     own = xall.at[xl, y, c]
     ag_x = remote(x_hbm, own, ag_s.at[0], ag_r.at[0], xother)
     ag_y0 = [remote(x_hbm, own, ag_s.at[1 + k], ag_r.at[1 + k], yother[k]) for k in range(3)]
-    ag_x.start()
+    w_near = remote(w_hbm.at[rest], wn.at[rest], wsem_s.at[0, 2], wsem_r.at[0, 2], near)
+    w_out = remote(w_hbm.at[rest], wo.at[rest], wsem_s.at[1, 2], wsem_r.at[1, 2], out)
+
+    def near_rows(blocks):
+        return [
+            remote(w_hbm.at[blk], wn.at[blk], wsem_s.at[0, i], wsem_r.at[0, i], near)
+            for i, blk in enumerate(blocks)
+        ]
+
+    def out_rows(blocks):
+        return [
+            remote(w_hbm.at[blk], wo.at[blk], wsem_s.at[1, i], wsem_r.at[1, i], out)
+            for i, blk in enumerate(blocks)
+        ]
+
+    def relays(blocks):
+        return [
+            remote(
+                wn.at[blk],
+                relw.at[pl.ds(blk.start - blocks[0].start, blk.size)],
+                rel_s.at[i],
+                rel_r.at[i],
+                across,
+            )
+            for i, blk in enumerate(blocks)
+        ]
+
+    def sums(blocks):
+        size = sum(blk.size for blk in blocks)
+        return remote(
+            relw.at[pl.ds(0, size)],
+            wn.at[pl.ds(blocks[0].start, size)],
+            rel_s.at[2],
+            rel_r.at[2],
+            near,
+        )
+
+    def pass_on(blocks, i):
+        near_rows(blocks)[i].wait_recv()
+        relays(blocks)[i].start()
+
+    def granted(i):
+        relays(outer_rows)[i].wait_recv()
+        for dev in outs:
+            pl.semaphore_signal(grants.at[i], inc=1, device_id=dev, device_id_type=MESH)
+        pl.semaphore_wait(grants.at[i], 2)
+
     for cp in ag_y0:
         cp.start()
-    w_near = remote(w_hbm.at[rest], wn.at[rest], wsem_s.at[0, 1], wsem_r.at[0, 1], near)
-    w_out = remote(w_hbm.at[rest], wo.at[rest], wsem_s.at[1, 1], wsem_r.at[1, 1], out)
-
-    def near_rows(blk):
-        return remote(w_hbm.at[blk], wn.at[blk], wsem_s.at[0, 0], wsem_r.at[0, 0], near)
-
-    def out_rows(blk):
-        return remote(w_hbm.at[blk], wo.at[blk], wsem_s.at[1, 0], wsem_r.at[1, 0], out)
-
-    def relay(blk):
-        return remote(wn.at[blk], relw.at[pl.ds(0, blk.size)], rel_s.at[0], rel_r.at[0], across)
-
-    def sums(blk):
-        return remote(relw.at[pl.ds(0, blk.size)], wn.at[blk], rel_s.at[1], rel_r.at[1], near)
-
-    def first_rows(mine, theirs):
-        near_rows(theirs).start()
-        out_rows(mine).start()
-
-    by_kind(first_rows)
-    w_near.start()
-    w_out.start()
+
+    @pl.when(inner)
+    def _():
+        ag_x.start()
+        for cp in near_rows(outer_rows) + out_rows(inner_rows) + [w_near, w_out]:
+            cp.start()
+
+    @pl.when(jnp.logical_not(inner))
+    def _():
+        out_rows(outer_rows)[0].start()
+        ag_x.start()
+        for cp in near_rows(inner_rows) + [w_near]:
+            cp.start()
 
     load_a.wait()
     load_h.wait()
@@ -112,11 +153,7 @@
     lax.fori_loop(0, tokens // 64, act, 0)
     load_m.start()
 
-    far = xall.at[1 - xl, y, c]
-    ag_x.wait_recv()
-    ag_y1 = [remote(far, far, ag_s.at[4 + k], ag_r.at[4 + k], yother[k]) for k in range(3)]
-    for cp in ag_y1:
-        cp.start()
+    pl.when(jnp.logical_not(inner))(lambda: pass_on(outer_rows, 0))
 
     load_w.wait()
 
@@ -130,11 +167,22 @@
 
     lax.fori_loop(0, chunks, cot, 0)
 
-    def pass_on(mine, theirs):
-        near_rows(mine).wait_recv()
-        relay(mine).start()
-
-    by_kind(pass_on)
+    far = xall.at[1 - xl, y, c]
+    ag_x.wait_recv()
+    ag_y1 = [remote(far, far, ag_s.at[4 + k], ag_r.at[4 + k], yother[k]) for k in range(3)]
+    for cp in ag_y1:
+        cp.start()
+
+    pl.when(inner)(lambda: pass_on(inner_rows, 0))
+
+    @pl.when(jnp.logical_not(inner))
+    def _():
+        relays(outer_rows)[0].wait_send()
+        out_rows(outer_rows)[1].start()
+        pass_on(outer_rows, 1)
+        granted(0)
+        w_out.start()
+
     rs_c = remote(part.at[:, 1 - c], crecv, rs_s.at[0], rs_r.at[0], cother)
 
     load_x.wait()
@@ -207,19 +255,22 @@
     lax.fori_loop(0, FIRST, early, 0)
     lax.fori_loop(FIRST, chunks, moments, 0)
 
-    def send_sum(mine, theirs):
-        relay(mine).wait_recv()
+    def send_sum(mine):
+        size = sum(blk.size for blk in mine)
 
         def add_own(i, _):
             here = pl.ds(pl.multiple_of(i * PIECE, PIECE), PIECE)
-            sub = pl.ds(pl.multiple_of(mine.start + i * PIECE, PIECE), PIECE)
+            sub = pl.ds(pl.multiple_of(mine[0].start + i * PIECE, PIECE), PIECE)
             relw[here] = (relw[here].astype(jnp.float32) + wv[sub].astype(jnp.float32)).astype(jnp.bfloat16)
             return 0
 
-        lax.fori_loop(0, mine.size // PIECE, add_own, 0)
+        lax.fori_loop(0, size // PIECE, add_own, 0)
         sums(mine).start()
 
-    pl.when(inner)(lambda: send_sum(inner_rows, outer_rows))
+    @pl.when(inner)
+    def _():
+        relays(inner_rows)[0].wait_recv()
+        send_sum(inner_rows)
 
     for cp in rs_y:
         cp.wait_recv()
@@ -239,32 +290,28 @@
 
     @pl.when(jnp.logical_not(inner))
     def _():
-        relay(outer_rows).wait_send()
-        send(0, chunks, send_out)
-        send_sum(outer_rows, inner_rows)
+        relays(outer_rows)[1].wait_send()
+        send(0, 1, send_out)
+        granted(1)
+        send(1, chunks, send_out)
+        send_sum(outer_rows)
         send(FIRST, chunks, send_near)
 
     w_near.wait_recv()
     w_out.wait_recv()
 
     def last_rows(mine, theirs):
-        out_rows(mine).wait_recv()
+        for cp in out_rows(mine):
+            cp.wait_recv()
         sums(theirs).wait_recv()
 
     by_kind(last_rows)
-    pl.when(inner)(lambda: relay(inner_rows).wait_send())
-    low = jnp.where(inner, INNER_ROWS, 0)
-    high = jnp.where(inner, INNER_ROWS + OUTER_ROWS, INNER_ROWS)
+    pl.when(inner)(lambda: relays(inner_rows)[0].wait_send())
+    low = jnp.where(inner, outer_rows[0].start, 0)
+    high = jnp.where(inner, rest.start, outer_rows[0].start)
 
     def fresh(w, f):
         return (w.astype(jnp.float32) - learn_rate * f).astype(jnp.bfloat16).astype(jnp.float32)
-
-    def outputs(n):
-        blk = rows_of(n)
-        return (
-            pltpu.make_async_copy(wn.at[blk], mw_hbm.at[blk], out_s.at[0, n]),
-            pltpu.make_async_copy(fn.at[blk], mm_hbm.at[blk], out_s.at[1, n]),
-        )
 
     def mix(n, _):
         blk = rows_of(n)
@@ -292,31 +339,23 @@
             return 0
 
         lax.fori_loop(0, CHUNK // PIECE, piece, 0)
-        for cp in outputs(n):
-            cp.start()
         return 0
 
     lax.fori_loop(0, LATE, mix, 0)
     rs_x.wait_recv()
     igv[...] = ((over_y(xl) + xrecv[...].astype(jnp.float32)) * scale).astype(jnp.bfloat16)
-    out_ig = pltpu.make_async_copy(igv, ig_hbm, loc.at[5])
-    out_ig.start()
     lax.fori_loop(LATE, chunks, mix, 0)
 
     def drain(n, _):
         blk = rows_of(n)
         send_near(blk, n).wait_send()
         send_out(blk, n).wait_send()
-        for cp in outputs(n):
-            cp.wait()
         return 0
 
     lax.fori_loop(0, chunks, drain, 0)
-    out_ig.wait()
     def sent(mine, theirs):
-        near_rows(theirs).wait_send()
-        out_rows(mine).wait_send()
-        sums(mine).wait_send()
+        for cp in near_rows(theirs) + out_rows(mine) + [sums(mine)]:
+            cp.wait_send()
 
     by_kind(sent)
     for cp in [ag_x, *ag_y0, *ag_y1, ag_c0, ag_c1, rs_c, *rs_y, rs_x, w_near, w_out]:
@@ -333,13 +372,9 @@
     big = pltpu.VMEM((depth, width), bf)
     ig, mw, mm = pl.pallas_call(
         kernel,
-        out_shape=(
-            jax.ShapeDtypeStruct((rows, depth), bf),
-            jax.ShapeDtypeStruct((depth, width), bf),
-            jax.ShapeDtypeStruct((depth, width), bf),
-        ),
+        out_shape=(pltpu.VMEM((rows, depth), bf), big, big),
         in_specs=[any_spec] * 5,
-        out_specs=(any_spec,) * 3,
+        out_specs=(pl.BlockSpec(memory_space=pltpu.VMEM),) * 3,
         scratch_shapes=[
             big,
             big,
@@ -350,27 +385,24 @@
             pltpu.VMEM((3, 2, rows, depth), bf),
             pltpu.VMEM((rows, depth), bf),
             pltpu.VMEM((rows, depth), bf),
-            pltpu.VMEM((rows, depth), bf),
             big,
             big,
-            big,
-            big,
-            pltpu.VMEM((max(INNER_ROWS, OUTER_ROWS), width), bf),
-            dma((6,)),
-            dma((2, 2)),
-            dma((2, 2)),
+            pltpu.VMEM((max(sum(INNER_ROWS), sum(OUTER_ROWS)), width), bf),
+            dma((5,)),
+            dma((2, 3)),
+            dma((2, 3)),
             dma((9,)),
             dma((9,)),
             dma((8,)),
             dma((8,)),
             dma((2, chunks)),
             dma((2, chunks)),
-            dma((2,)),
-            dma((2,)),
-            dma((2, chunks)),
+            dma((3,)),
+            dma((3,)),
+            pltpu.SemaphoreType.REGULAR((2,)),
         ],
         compiler_params=pltpu.CompilerParams(
-            collective_id=0, has_side_effects=True, vmem_limit_bytes=62 * 2**20
+            collective_id=0, has_side_effects=True, vmem_limit_bytes=50 * 2**20
         ),
         name="step",
     )(inputs, gate_pre, grad_hidden, up_weight[0], momentum[0])

time: 224 us -> 218 us (0.973)
  local copies, waits for them, and re-layouts: 9 us -> 5.07 us
    unnamed x7 -> x3, local copies, waits for them, and re-layouts: 9 us -> 5.07 us
where the time goes in v3:
time: 218 us
  Pallas kernels  212 us (97%)
  local copies, waits for them, and re-layouts  5.07 us (2%)
    pallas_call x1, Pallas kernels, per_device(): pl.pallas_call(kernel, out_shape=(pltpu.VMEM((rows, depth), bf), big, big...  212 us
    unnamed x3, local copies, waits for them, and re-layouts  5.07 us

profile of v3, /device:TPU:0, one launch (start us, length us, event | category | flops | bytes accessed | tf_op | source)
XLA Modules:
  0.0 218.2 jit_solution(13717328924403814766)
XLA Ops:
  0.6 212.5 %step.1 = (bf16[96,2560]{1,0:T(8,128)(2,1)S(1)}, bf16[2560,896]{1,0:T(8,128)(2,1)S(1)}, bf16[2560,896]{1,0:T(8,128)(2,1)S(1)}) custom-call(bf16[96,2560]{1,0:T(8,128)(2,1)} %x_hbm.1, bf16[1536,896]{1,0:T(8,128)(2,1)} %a_hbm.1, bf16[1536,896]{1,0:T(8,128)(2,1)} %h_hbm.1, bf16[2560,896]{1,0:T(8,128)(2,1)} %bitcast.6, bf16[2560,896]{1,0:T(8,128)(2,1)} %bitcast.7), custom_call_target="tpu_custom_call" | custom-call | tf_op jit(solution)/shard_map/step/pallas_call | solution.py:373
  213.1 0.8 copy.11
  213.9 2.1 copy.12
  216.0 2.1 copy.13

commit v4 on v3

--- a/solution.py
+++ b/solution.py
@@ -8,18 +8,20 @@
 momentum_beta = 0.9
 learn_rate = 0.1
 CHUNK = 256
-INNER_ROWS = (640,)
-OUTER_ROWS = (288, 320)
+SEND = 128
+INNER_ROWS = (608,)
+OUTER_ROWS = (256, 256)
 PIECE = 32
-FIRST = 4
-LATE = 7
+FIRST = 8
+LATE = 14
+BURST = 2
 MESH = pl.DeviceIdType.MESH
 
 
 def kernel(
     x_hbm, a_hbm, h_hbm, w_hbm, m_hbm,
     igv, wn, fn,
-    wv, fv, g, xall, part, crecv, yrecv, xsend, xrecv, wo, fo,
+    wv, fv, g, xall, part, crecv, yrecv, tup, tdown, xsend, xrecv, wo, fo,
     relw,
     loc, wsem_s, wsem_r, ag_s, ag_r, rs_s, rs_r, f_s, f_r, rel_s, rel_r, grants,
 ):
@@ -27,14 +29,17 @@
     rows = x_hbm.shape[0]
     tokens = g.shape[0]
     chunks = depth // CHUNK
+    sends = depth // SEND
     scale = depth ** (-0.5)
     rep = lax.axis_index("rep")
     tp = lax.axis_index("tp")
     c = lax.rem(tp, 2)
     y = lax.rem(lax.div(tp, 2), 4)
     xl = lax.div(tp, 8)
-    yo = [lax.rem(y + k, 4) for k in (1, 2, 3)]
-    yother = [(rep, xl * 8 + yk * 2 + c) for yk in yo]
+    yu, yd = lax.rem(y + 1, 4), lax.rem(y + 3, 4)
+    yup, ydown = [(rep, xl * 8 + yk * 2 + c) for yk in (yu, yd)]
+    half = rows // 2
+    lower, upper = pl.ds(0, half), pl.ds(half, half)
     odd = lax.rem(rep, 2)
     quad = lax.rem(rep, 4)
     inner = jnp.logical_or(quad == 1, quad == 2)
@@ -71,13 +76,26 @@
     load_x.start()
 
     barrier = pltpu.get_barrier_semaphore()
-    for dev in [near, *outs, across, xother, cother] + yother:
+    for dev in [near, *outs, across, xother, cother, yup, ydown]:
         pl.semaphore_signal(barrier, inc=1, device_id=dev, device_id_type=MESH)
-    pl.semaphore_wait(barrier, 9)
+    pl.semaphore_wait(barrier, 8)
 
     own = xall.at[xl, y, c]
     ag_x = remote(x_hbm, own, ag_s.at[0], ag_r.at[0], xother)
-    ag_y0 = [remote(x_hbm, own, ag_s.at[1 + k], ag_r.at[1 + k], yother[k]) for k in range(3)]
+    ag_y0 = [
+        remote(x_hbm, own, ag_s.at[1], ag_r.at[1], yup),
+        remote(x_hbm, own, ag_s.at[2], ag_r.at[2], ydown),
+    ]
+
+    def passed(u, i):
+        from_down, from_up = xall.at[u, yd, c, lower], xall.at[u, yu, c, upper]
+        return [
+            remote(from_down, from_down, ag_s.at[i], ag_r.at[i], yup),
+            remote(from_up, from_up, ag_s.at[i + 1], ag_r.at[i + 1], ydown),
+        ]
+
+    ag_y0p = passed(xl, 3)
+    ag_y1p = passed(1 - xl, 7)
     w_near = remote(w_hbm.at[rest], wn.at[rest], wsem_s.at[0, 2], wsem_r.at[0, 2], near)
     w_out = remote(w_hbm.at[rest], wo.at[rest], wsem_s.at[1, 2], wsem_r.at[1, 2], out)
 
@@ -155,6 +173,11 @@
 
     pl.when(jnp.logical_not(inner))(lambda: pass_on(outer_rows, 0))
 
+    for cp in ag_y0:
+        cp.wait_recv()
+    for cp in ag_y0p:
+        cp.start()
+
     load_w.wait()
 
     def cot(n, _):
@@ -162,14 +185,19 @@
         res = lax.dot_general(
             g[...], wv[cols], (((1,), (1,)), ((), ())), preferred_element_type=jnp.float32
         )
-        part[:, :, :, cols] = res.astype(jnp.bfloat16).reshape(8, 2, rows, CHUNK)
+        part[:, :, :, :, cols] = res.astype(jnp.bfloat16).reshape(2, 4, 2, rows, CHUNK)
         return 0
 
     lax.fori_loop(0, chunks, cot, 0)
+    rs_c = remote(part.at[:, :, 1 - c], crecv, rs_s.at[0], rs_r.at[0], cother)
+    rs_c.start()
 
     far = xall.at[1 - xl, y, c]
     ag_x.wait_recv()
-    ag_y1 = [remote(far, far, ag_s.at[4 + k], ag_r.at[4 + k], yother[k]) for k in range(3)]
+    ag_y1 = [
+        remote(far, far, ag_s.at[5], ag_r.at[5], yup),
+        remote(far, far, ag_s.at[6], ag_r.at[6], ydown),
+    ]
     for cp in ag_y1:
         cp.start()
 
@@ -183,37 +211,50 @@
         granted(0)
         w_out.start()
 
-    rs_c = remote(part.at[:, 1 - c], crecv, rs_s.at[0], rs_r.at[0], cother)
-
     load_x.wait()
-    for cp in ag_y0:
-        cp.wait_recv()
-    ag_c0 = remote(xall.at[xl, :, c], xall.at[xl, :, c], ag_s.at[7], ag_r.at[7], cother)
+    for cp in ag_y0p:
+        cp.wait_recv()
+    ag_c0 = remote(xall.at[xl, :, c], xall.at[xl, :, c], ag_s.at[9], ag_r.at[9], cother)
     ag_c0.start()
-    rs_c.start()
     for cp in ag_y1:
         cp.wait_recv()
-    ag_c1 = remote(xall.at[1 - xl, :, c], xall.at[1 - xl, :, c], ag_s.at[8], ag_r.at[8], cother)
-    ag_c1.start()
+    for cp in ag_y1p:
+        cp.start()
 
     rs_c.wait_recv()
 
     def add_core(b, _):
         u, v = lax.div(b, 4), lax.rem(b, 4)
-        crecv[b] = (part[b, c].astype(jnp.float32) + crecv[b].astype(jnp.float32)).astype(jnp.bfloat16)
+        total = part[u, v, c].astype(jnp.float32) + crecv[u, v].astype(jnp.float32)
+        crecv[u, v] = total.astype(jnp.bfloat16)
         return 0
 
     lax.fori_loop(0, 8, add_core, 0)
-    rs_y = []
-    for k in range(3):
-        for u in range(2):
-            j = 1 + 2 * k + u
-            rs_y.append(
-                remote(crecv.at[4 * u + yo[k]], yrecv.at[k, u], rs_s.at[j], rs_r.at[j], yother[k])
-            )
-    for cp in rs_y:
-        cp.start()
-
+
+    far_y = lax.rem(y + 2, 4)
+
+    def scatter(src, dst, i, dev):
+        return remote(src, dst, rs_s.at[i], rs_r.at[i], dev)
+
+    transit = [
+        scatter(crecv.at[:, far_y, lower], tup, 1, yup),
+        scatter(crecv.at[:, far_y, upper], tdown, 2, ydown),
+    ]
+    ready = [
+        scatter(crecv.at[:, yu, upper], yrecv.at[0, :, upper], 3, yup),
+        scatter(crecv.at[:, yd, lower], yrecv.at[1, :, lower], 4, ydown),
+    ]
+    joined = [
+        scatter(crecv.at[:, yu, lower], yrecv.at[0, :, lower], 5, yup),
+        scatter(crecv.at[:, yd, upper], yrecv.at[1, :, upper], 6, ydown),
+    ]
+    for cp in transit + ready:
+        cp.start()
+
+    for cp in ag_y1p:
+        cp.wait_recv()
+    ag_c1 = remote(xall.at[1 - xl, :, c], xall.at[1 - xl, :, c], ag_s.at[10], ag_r.at[10], cother)
+    ag_c1.start()
     ag_c0.wait_recv()
     ag_c1.wait_recv()
     load_m.wait()
@@ -231,11 +272,11 @@
         )
         fv[blk] = (momentum_beta * fv[blk].astype(jnp.float32) + delta * scale).astype(jnp.bfloat16)
 
-    def rows_of(n):
-        return pl.ds(pl.multiple_of(n * CHUNK, CHUNK), CHUNK)
+    def rows_of(n, size=SEND):
+        return pl.ds(pl.multiple_of(n * size, size), size)
 
     def moments(n, _):
-        moment(rows_of(n))
+        moment(rows_of(n, CHUNK))
         return 0
 
     def send(lo, hi, *ways):
@@ -248,12 +289,27 @@
 
     def early(n, _):
         moments(n, 0)
-        send_near(rows_of(n), n).start()
-        pl.when(inner)(lambda: send_out(rows_of(n), n).start())
-        return 0
-
-    lax.fori_loop(0, FIRST, early, 0)
-    lax.fori_loop(FIRST, chunks, moments, 0)
+        for i in range(CHUNK // SEND):
+            block = n * (CHUNK // SEND) + i
+            send_near(rows_of(block), block).start()
+            pl.when(inner)(lambda: send_out(rows_of(block), block).start())
+        return 0
+
+    lax.fori_loop(0, FIRST * SEND // CHUNK, early, 0)
+
+    for cp in transit:
+        cp.wait_recv()
+    for u in range(2):
+        crecv[u, yu, lower] = (
+            crecv[u, yu, lower].astype(jnp.float32) + tup[u].astype(jnp.float32)
+        ).astype(jnp.bfloat16)
+        crecv[u, yd, upper] = (
+            crecv[u, yd, upper].astype(jnp.float32) + tdown[u].astype(jnp.float32)
+        ).astype(jnp.bfloat16)
+    for cp in joined:
+        cp.start()
+
+    lax.fori_loop(FIRST * SEND // CHUNK, chunks, moments, 0)
 
     def send_sum(mine):
         size = sum(blk.size for blk in mine)
@@ -272,30 +328,30 @@
         relays(inner_rows)[0].wait_recv()
         send_sum(inner_rows)
 
-    for cp in rs_y:
+    for cp in ready + joined:
         cp.wait_recv()
 
     def over_y(u):
         return (
-            crecv[4 * u + y].astype(jnp.float32)
+            crecv[u, y].astype(jnp.float32)
             + yrecv[0, u].astype(jnp.float32)
             + yrecv[1, u].astype(jnp.float32)
-            + yrecv[2, u].astype(jnp.float32)
         )
 
     xsend[...] = over_y(1 - xl).astype(jnp.bfloat16)
     rs_x = remote(xsend, xrecv, rs_s.at[7], rs_r.at[7], xother)
+    pl.when(jnp.logical_not(inner))(lambda: w_out.wait_send())
     rs_x.start()
-    pl.when(inner)(lambda: send(FIRST, chunks, send_near, send_out))
+    pl.when(inner)(lambda: send(FIRST, sends, send_near, send_out))
 
     @pl.when(jnp.logical_not(inner))
     def _():
         relays(outer_rows)[1].wait_send()
-        send(0, 1, send_out)
+        send(0, BURST, send_out)
         granted(1)
-        send(1, chunks, send_out)
+        send(BURST, sends, send_out)
         send_sum(outer_rows)
-        send(FIRST, chunks, send_near)
+        send(FIRST, sends, send_near)
 
     w_near.wait_recv()
     w_out.wait_recv()
@@ -306,7 +362,12 @@
         sums(theirs).wait_recv()
 
     by_kind(last_rows)
-    pl.when(inner)(lambda: relays(inner_rows)[0].wait_send())
+
+    @pl.when(inner)
+    def _():
+        relays(inner_rows)[0].wait_send()
+        w_out.wait_send()
+
     low = jnp.where(inner, outer_rows[0].start, 0)
     high = jnp.where(inner, rest.start, outer_rows[0].start)
 
@@ -319,7 +380,7 @@
         send_out(blk, n).wait_recv()
 
         def piece(i, _):
-            start = n * CHUNK + i * PIECE
+            start = n * SEND + i * PIECE
             sub = pl.ds(pl.multiple_of(start, PIECE), PIECE)
             summed = jnp.logical_and(start >= low, start < high)
             f0, f1, f2 = (r[sub].astype(jnp.float32) for r in (fn, fv, fo))
@@ -338,13 +399,13 @@
             fn[sub] = ((f0 + f1 + f2) * (1.0 / 3.0)).astype(jnp.bfloat16)
             return 0
 
-        lax.fori_loop(0, CHUNK // PIECE, piece, 0)
+        lax.fori_loop(0, SEND // PIECE, piece, 0)
         return 0
 
     lax.fori_loop(0, LATE, mix, 0)
     rs_x.wait_recv()
     igv[...] = ((over_y(xl) + xrecv[...].astype(jnp.float32)) * scale).astype(jnp.bfloat16)
-    lax.fori_loop(LATE, chunks, mix, 0)
+    lax.fori_loop(LATE, sends, mix, 0)
 
     def drain(n, _):
         blk = rows_of(n)
@@ -352,20 +413,21 @@
         send_out(blk, n).wait_send()
         return 0
 
-    lax.fori_loop(0, chunks, drain, 0)
+    lax.fori_loop(0, sends, drain, 0)
     def sent(mine, theirs):
         for cp in near_rows(theirs) + out_rows(mine) + [sums(mine)]:
             cp.wait_send()
 
     by_kind(sent)
-    for cp in [ag_x, *ag_y0, *ag_y1, ag_c0, ag_c1, rs_c, *rs_y, rs_x, w_near, w_out]:
+    gathers = [ag_x, *ag_y0, *ag_y0p, *ag_y1, *ag_y1p, ag_c0, ag_c1]
+    for cp in gathers + [rs_c, *transit, *ready, *joined, rs_x, w_near]:
         cp.wait_send()
 
 
 def per_device(inputs, gate_pre, grad_hidden, up_weight, momentum):
     rows, depth = inputs.shape
     tokens, width = gate_pre.shape
-    chunks = depth // CHUNK
+    sends = depth // SEND
     bf = jnp.bfloat16
     any_spec = pl.BlockSpec(memory_space=pl.ANY)
     dma = pltpu.SemaphoreType.DMA
@@ -380,9 +442,11 @@
             big,
             pltpu.VMEM((tokens, width), bf),
             pltpu.VMEM((2, 4, 2, rows, depth), bf),
-            pltpu.VMEM((8, 2, rows, depth), bf),
-            pltpu.VMEM((8, rows, depth), bf),
-            pltpu.VMEM((3, 2, rows, depth), bf),
+            pltpu.VMEM((2, 4, 2, rows, depth), bf),
+            pltpu.VMEM((2, 4, rows, depth), bf),
+            pltpu.VMEM((2, 2, rows, depth), bf),
+            pltpu.VMEM((2, rows // 2, depth), bf),
+            pltpu.VMEM((2, rows // 2, depth), bf),
             pltpu.VMEM((rows, depth), bf),
             pltpu.VMEM((rows, depth), bf),
             big,
@@ -391,12 +455,12 @@
             dma((5,)),
             dma((2, 3)),
             dma((2, 3)),
-            dma((9,)),
-            dma((9,)),
+            dma((11,)),
+            dma((11,)),
             dma((8,)),
             dma((8,)),
-            dma((2, chunks)),
-            dma((2, chunks)),
+            dma((2, sends)),
+            dma((2, sends)),
             dma((3,)),
             dma((3,)),
             pltpu.SemaphoreType.REGULAR((2,)),

time: 218 us -> 214 us (0.982)
  Pallas kernels: 212 us -> 208 us
    pallas_call x1, Pallas kernels: 212 us -> 208 us  [per_device(): pl.pallas_call(kernel, out_shape=(pltpu.VMEM((rows, depth), bf), big, big...]
where the time goes in v4:
time: 214 us
  Pallas kernels  208 us (97%)
  local copies, waits for them, and re-layouts  5.07 us (2%)
    pallas_call x1, Pallas kernels, per_device(): pl.pallas_call(kernel, out_shape=(pltpu.VMEM((rows, depth), bf), big, big...  208 us
    unnamed x3, local copies, waits for them, and re-layouts  5.07 us

profile of v4, /device:TPU:0, one launch (start us, length us, event | category | flops | bytes accessed | tf_op | source)
XLA Modules:
  0.0 213.9 jit_solution(6409464323641084582)
XLA Ops:
  0.6 208.2 %step.1 = (bf16[96,2560]{1,0:T(8,128)(2,1)S(1)}, bf16[2560,896]{1,0:T(8,128)(2,1)S(1)}, bf16[2560,896]{1,0:T(8,128)(2,1)S(1)}) custom-call(bf16[96,2560]{1,0:T(8,128)(2,1)} %x_hbm.1, bf16[1536,896]{1,0:T(8,128)(2,1)} %a_hbm.1, bf16[1536,896]{1,0:T(8,128)(2,1)} %h_hbm.1, bf16[2560,896]{1,0:T(8,128)(2,1)} %bitcast.6, bf16[2560,896]{1,0:T(8,128)(2,1)} %bitcast.7), custom_call_target="tpu_custom_call" | custom-call | tf_op jit(solution)/shard_map/step/pallas_call | solution.py:435
  208.8 0.8 copy.11
  209.6 2.1 %copy.12 = bf16[1,2560,896]{2,1,0:T(8,128)(2,1)} copy(bf16[1,2560,896]{2,1,0:T(8,128)(2,1)S(1)} %bitcast.5) | data formatting | bytes 9175040
  211.7 2.1 %copy.13 = bf16[1,2560,896]{2,1,0:T(8,128)(2,1)} copy(bf16[1,2560,896]{2,1,0:T(8,128)(2,1)S(1)} %bitcast.4) | data formatting | bytes 9175040

commit v5 on v4

--- a/solution.py
+++ b/solution.py
@@ -14,6 +14,7 @@
 PIECE = 32
 FIRST = 8
 LATE = 14
+STORES = 4
 BURST = 2
 MESH = pl.DeviceIdType.MESH
 
@@ -422,6 +423,19 @@
     gathers = [ag_x, *ag_y0, *ag_y0p, *ag_y1, *ag_y1p, ag_c0, ag_c1]
     for cp in gathers + [rs_c, *transit, *ready, *joined, rs_x, w_near]:
         cp.wait_send()
+
+
+def store(ig, mw, mm, ig_hbm, mw_hbm, mm_hbm, sem):
+    copies = [pltpu.make_async_copy(ig, ig_hbm, sem.at[0])]
+    part = mw.shape[0] // STORES
+    for i in range(STORES):
+        blk = pl.ds(i * part, part)
+        copies.append(pltpu.make_async_copy(mw.at[blk], mw_hbm.at[blk], sem.at[1 + 2 * i]))
+        copies.append(pltpu.make_async_copy(mm.at[blk], mm_hbm.at[blk], sem.at[2 + 2 * i]))
+    for cp in copies:
+        cp.start()
+    for cp in copies:
+        cp.wait()
 
 
 def per_device(inputs, gate_pre, grad_hidden, up_weight, momentum):
@@ -470,6 +484,16 @@
         ),
         name="step",
     )(inputs, gate_pre, grad_hidden, up_weight[0], momentum[0])
+    whole = jax.ShapeDtypeStruct((depth, width), bf)
+    ig, mw, mm = pl.pallas_call(
+        store,
+        out_shape=(jax.ShapeDtypeStruct((rows, depth), bf), whole, whole),
+        in_specs=[any_spec] * 3,
+        out_specs=(any_spec,) * 3,
+        scratch_shapes=[dma((1 + 2 * STORES,))],
+        compiler_params=pltpu.CompilerParams(vmem_limit_bytes=2**20),
+        name="store",
+    )(ig, mw, mm)
     return ig, mw[None], mm[None]
 
 

time: 214 us -> 213 us (level)
  local copies, waits for them, and re-layouts: 5.07 us -> 0 us
  Pallas kernels: 208 us -> 212 us
    unnamed x3 -> x0, local copies, waits for them, and re-layouts: 5.07 us -> none
    pallas_call x0 -> x1, Pallas kernels: none -> 3.79 us  [per_device(): pl.pallas_call(store, out_shape=(jax.ShapeDtypeStruct((rows, depth), bf),...]
where the time goes in v5:
time: 213 us
  Pallas kernels  212 us (100%)
    pallas_call x1, Pallas kernels, per_device(): pl.pallas_call(kernel, out_shape=(pltpu.VMEM((rows, depth), bf), big, big...  208 us

profile of v5, /device:TPU:0, one launch (start us, length us, event | category | flops | bytes accessed | tf_op | source)
XLA Modules:
  0.0 212.6 jit_solution(9179081711052789014)
XLA Ops:
  0.6 208.2 %step.1 = (bf16[96,2560]{1,0:T(8,128)(2,1)S(1)}, bf16[2560,896]{1,0:T(8,128)(2,1)S(1)}, bf16[2560,896]{1,0:T(8,128)(2,1)S(1)}) custom-call(bf16[96,2560]{1,0:T(8,128)(2,1)} %x_hbm.1, bf16[1536,896]{1,0:T(8,128)(2,1)} %a_hbm.1, bf16[1536,896]{1,0:T(8,128)(2,1)} %h_hbm.1, bf16[2560,896]{1,0:T(8,128)(2,1)} %bitcast.4, bf16[2560,896]{1,0:T(8,128)(2,1)} %bitcast.5), custom_call_target="tpu_custom_call" | custom-call | tf_op jit(solution)/shard_map/step/pallas_call | solution.py:449
  208.8 3.8 %store.1 = (bf16[96,2560]{1,0:T(8,128)(2,1)}, bf16[2560,896]{1,0:T(8,128)(2,1)}, bf16[2560,896]{1,0:T(8,128)(2,1)}) custom-call(bf16[96,2560]{1,0:T(8,128)(2,1)S(1)} %get-tuple-element.9.ig, bf16[2560,896]{1,0:T(8,128)(2,1)S(1)} %get-tuple-element.10.mw, bf16[2560,896]{1,0:T(8,128)(2,1)S(1)} %get-tuple-element.11.mm), custom_call_target="tpu_custom_call" | custom-call | tf_op jit(solution)/shard_map/store/pallas_call | solution.py:488

commit v6 on v5

--- a/solution.py
+++ b/solution.py
@@ -9,9 +9,9 @@
 learn_rate = 0.1
 CHUNK = 256
 SEND = 128
-INNER_ROWS = (608,)
-OUTER_ROWS = (256, 256)
-PIECE = 32
+INNER_ROWS = (624,)
+OUTER_ROWS = (256, 272)
+PIECE = 16
 FIRST = 8
 LATE = 14
 STORES = 4

time: 213 us -> 212 us (level)
  no operation moved by 1% of the time
where the time goes in v6:
time: 212 us
  Pallas kernels  211 us (100%)
    pallas_call x1, Pallas kernels, per_device(): pl.pallas_call(kernel, out_shape=(pltpu.VMEM((rows, depth), bf), big, big...  208 us

profile of v6, /device:TPU:0, one launch (start us, length us, event | category | flops | bytes accessed | tf_op | source)
XLA Modules:
  0.0 212.0 jit_solution(5414898801935269753)
XLA Ops:
  0.6 207.6 %step.1 = (bf16[96,2560]{1,0:T(8,128)(2,1)S(1)}, bf16[2560,896]{1,0:T(8,128)(2,1)S(1)}, bf16[2560,896]{1,0:T(8,128)(2,1)S(1)}) custom-call(bf16[96,2560]{1,0:T(8,128)(2,1)} %x_hbm.1, bf16[1536,896]{1,0:T(8,128)(2,1)} %a_hbm.1, bf16[1536,896]{1,0:T(8,128)(2,1)} %h_hbm.1, bf16[2560,896]{1,0:T(8,128)(2,1)} %bitcast.4, bf16[2560,896]{1,0:T(8,128)(2,1)} %bitcast.5), custom_call_target="tpu_custom_call" | custom-call | tf_op jit(solution)/shard_map/step/pallas_call | solution.py:449
  208.2 3.8 %store.1 = (bf16[96,2560]{1,0:T(8,128)(2,1)}, bf16[2560,896]{1,0:T(8,128)(2,1)}, bf16[2560,896]{1,0:T(8,128)(2,1)}) custom-call(bf16[96,2560]{1,0:T(8,128)(2,1)S(1)} %get-tuple-element.9.ig, bf16[2560,896]{1,0:T(8,128)(2,1)S(1)} %get-tuple-element.10.mw, bf16[2560,896]{1,0:T(8,128)(2,1)S(1)} %get-tuple-element.11.mm), custom_call_target="tpu_custom_call" | custom-call | tf_op jit(solution)/shard_map/store/pallas_call | solution.py:488
